TPU v7x, 256 devices: a whole 4x4x8 slice. The times are simulated.
256 devices in a mesh: row: 8 (over y, core), col: 32 (over x, z).
Axes of the slice: x: 4, y: 4, z: 8, core: 2. Of those that a mesh axis runs over, the one named last changes fastest.
Arguments:
- slab: float32 [12288, 20480], P('row', 'col'), may hold values from -6 to 6
- reflectors: bfloat16 [4, 32, 256, 128], P(None, 'col'), may hold values from -0.375 to 0.375
- wy_factors: bfloat16 [4, 32, 128, 128], P(None, 'col'), as said below
- offsets: int32 [4, 32], replicated, may hold values from 0 to 12032, as said below
- band_owner: int32 [4, 32], replicated, may hold values from 0 to 31, each once within a row
Outputs:
- back_vectors: float32 [12288, 20480], P('row', 'col')
Inputs may be any that keep to these rules, and one draw needn't show every extreme that they name: In each sweep the offsets rise, each block's 256 rows end before the next block begins, the first block begins at row 0 and the last ends at row 12288; each multiple of 1536 strictly between 0 and 12288 lies strictly inside one block. `band_owner`: each row is a permutation of 0 to 31. `wy_factors`: each factor is upper triangular.
All inputs are finite; a program needn't handle non-finite values.
Results may differ from a plain program's by a relative error of at most 0.0003.
Values may be sent and summed in bfloat16 or wider, within the bound.
A program may use at most 128 MiB of HBM per device.

v0:
```python
import jax
import jax.numpy as jnp
from jax import lax
from jax.sharding import PartitionSpec as P

SWEEPS = 4


def with_halo(cells, sides, width):
    for axis, dim in sides:
        count = lax.axis_size(axis)
        ends = count - 1
        head = lax.slice_in_dim(cells, 0, width, axis=dim)
        tail = lax.slice_in_dim(cells, cells.shape[dim] - width, cells.shape[dim], axis=dim)
        cells = jnp.concatenate(
            [
                lax.ppermute(tail, axis, [(i, (i + 1) % count) for i in range(ends)]),
                cells,
                lax.ppermute(head, axis, [((i + 1) % count, i) for i in range(ends)]),
            ],
            axis=dim,
        )
    return cells


def fetch_blocks(local_refl, local_factor):
    gathered_refl, gathered_factor = (
        lax.all_gather(local_refl, "col", axis=0, tiled=True),
        lax.all_gather(local_factor, "col", axis=0, tiled=True),
    )
    return (gathered_refl, gathered_factor)


def on_device(slab, reflectors, wy_factors, offsets, band_owner):
    row_count, col_count = slab.shape
    block_width = wy_factors.shape[-1]
    span_rows = reflectors.shape[2]
    block_count = offsets.shape[1]
    slot_count = row_count // span_rows + 1
    tile_count = row_count // block_width
    highest = lax.Precision.HIGHEST
    row_start = lax.axis_index("row") * row_count
    global_rows = row_start + jnp.arange(row_count, dtype=jnp.int32)
    block_ids = jnp.arange(block_count, dtype=jnp.int32)
    state = slab
    for sweep_index in range(SWEEPS):
        all_refl, all_factor = fetch_blocks(reflectors[sweep_index], wy_factors[sweep_index])
        begins = offsets[sweep_index]
        owners = band_owner[sweep_index]
        inside = (
            (global_rows[:, None] >= begins[None, :])
            & (global_rows[:, None] < begins[None, :] + span_rows)
        ).astype(jnp.int32)
        covered = jnp.sum(inside, axis=1) > 0
        which_block = jnp.sum(inside * block_ids[None, :], axis=1)
        position = jnp.sum(inside * (global_rows[:, None] - begins[None, :]), axis=1)
        holders = jnp.sum(inside * owners[None, :], axis=1)
        first_block = jnp.sum((begins + span_rows <= row_start).astype(jnp.int32))
        touching = jnp.sum(
            ((begins < row_start + row_count) & (begins + span_rows > row_start)).astype(jnp.int32)
        )
        last_slot = jnp.maximum(touching - 1, 0)
        slot_index = jnp.clip(which_block - first_block, 0, slot_count - 1)
        flat_rows = all_refl.reshape(block_count * span_rows, block_width)
        refl_rows = jnp.where(
            covered[:, None], flat_rows[holders * span_rows + position].astype(jnp.float32), 0.0
        )
        slot_blocks = jnp.minimum(
            first_block + jnp.arange(slot_count, dtype=jnp.int32), block_count - 1
        )
        slot_owner = jnp.sum(
            (slot_blocks[:, None] == block_ids[None, :]).astype(jnp.int32) * owners[None, :], axis=1
        )
        slot_factor = all_factor[slot_owner].astype(jnp.float32)
        tile_slots = slot_index.reshape(tile_count, block_width)
        tile_cover = covered.reshape(tile_count, block_width)
        tile_base = jnp.minimum(
            jnp.min(jnp.where(tile_cover, tile_slots, slot_count), axis=1), slot_count - 1
        )
        half_index = tile_slots - tile_base[:, None]
        tile_masks = jnp.stack(
            [tile_cover & (half_index == 0), tile_cover & (half_index == 1)], axis=1
        ).astype(jnp.float32)
        reflector_tiles = (
            refl_rows.reshape(tile_count, 1, block_width, block_width) * tile_masks[..., None]
        )
        slab_tiles = state.reshape(tile_count, block_width, col_count)
        partial_value = jnp.einsum("tjrn,trc->tjnc", reflector_tiles, slab_tiles, precision=highest)
        halves = jnp.arange(2, dtype=jnp.int32)
        slots_all = jnp.arange(slot_count, dtype=jnp.int32)
        selector = (
            tile_base[:, None, None] + halves[None, :, None] == slots_all[None, None, :]
        ).astype(jnp.float32)
        inner_sums = jnp.einsum("tjk,tjnc->knc", selector, partial_value, precision=highest)
        edge_sums = jnp.stack([inner_sums[0], inner_sums[last_slot]])
        padded = with_halo(edge_sums, (("row", 0),), 1)
        first_clamp = jnp.minimum(first_block, block_count - 1)
        last_clamp = jnp.minimum(first_block + last_slot, block_count - 1)
        from_before = (touching > 0) & (begins[first_clamp] < row_start)
        from_after = (touching > 0) & (begins[last_clamp] + span_rows > row_start + row_count)
        inner_sums = inner_sums.at[0].add(jnp.where(from_before, padded[0], 0.0))
        inner_sums = inner_sums.at[last_slot].add(jnp.where(from_after, padded[3], 0.0))
        scaled = jnp.einsum("knm,kmc->knc", slot_factor, inner_sums, precision=highest)
        spread = jnp.einsum("tjk,knc->tjnc", selector, scaled, precision=highest)
        slab_tiles = slab_tiles - jnp.einsum(
            "tjrn,tjnc->trc", reflector_tiles, spread, precision=highest
        )
        state = slab_tiles.reshape(row_count, col_count)
    return state


def solution(mesh):
    placed = (P("row", "col"), P(None, "col", None, None), P(None, "col", None, None), P(), P())
    return jax.shard_map(
        on_device, mesh=mesh, in_specs=placed, out_specs=P("row", "col"), check_vma=False
    )
```

profile of v0, /device:TPU:1, one launch (start us, length us, event | category | flops | bytes accessed | tf_op | source)
XLA Modules:
  0.0 683.1 jit_solution(5291082509214520843)
XLA Ops:
  42.9 44.9 %all-gather.17.cloned.1.call-done = bf16[32,1,256,128]{3,2,1,0:T(8,128)(2,1)} async-done(((bf16[1,1,256,128]{3,2,1,0:T(8,128)(2,1)}), bf16[32,1,256,128]{3,2,1,0:T(8,128)(2,1)}) %all-gather.17.cloned.1.call-update) | async-done | bytes 2097168 | tf_op jit(solution)/shard_map/all_gather | solution.py:28
  87.8 4.7 gather_fusion
  93.7 10.3 %fusion.49 = f32[12,2,128,640]{3,2,1,0:T(8,128)S(1)} fusion(f32[12,128,640,1]{2,1,3,0:T(8,128)} %bitcast.226, f32[12,2,128]{2,1,0:T(2,128)S(1)} %copy.34, f32[12,128,128]{2,1,0:T(8,128)S(1)} %convert_select_fusion.3), kind=kOutput, calls=%fused_computation.61 | convolution fusion | flops 3020292096 | bytes 12595200 | tf_op jit(solution)/shard_map/tjrn,trc->tjnc/dot_general | solution.py:88
  103.9 8.2 %fusion.67 = f32[7,128,640]{2,0,1:T(8,128)S(1)} fusion(f32[12,2,128,640]{3,2,1,0:T(8,128)S(1)} %fusion.49, s32[12,2]{0,1:T(2,128)S(1)} %iota_add_fusion.4), kind=kOutput, calls=%fused_computation.63 | convolution fusion | flops 165150880 | bytes 10158176 | tf_op jit(solution)/shard_map/tjk,tjnc->knc/dot_general | solution.py:94
  112.4 7.6 %collective-permute-start = (f32[1,128,640]{2,0,1:T(1,128)S(1)}, f32[1,128,640]{2,0,1:T(1,128)S(1)}, u32[]{:S(2)}, u32[]{:S(2)}) collective-permute-start(f32[1,128,640]{2,0,1:T(1,128)S(1)} %constant_dynamic-slice_fusion.10), channel_id=1, source_target_pairs={{0,32},{32,64},{64,96},{96,128},{128,160},{160,192},{192,224},{1,3... | collective-permute-start | bytes 983048 | tf_op jit(solution)/shard_map/ppermute | solution.py:17
  120.0 4.0 collective-permute-done
  127.3 35.9 %all-gather.19.cloned.1.call-done = bf16[32,1,128,128]{3,2,1,0:T(8,128)(2,1)} async-done(((bf16[1,1,128,128]{3,2,1,0:T(8,128)(2,1)}), bf16[32,1,128,128]{3,2,1,0:T(8,128)(2,1)}) %all-gather.19.cloned.1.call-update) | async-done | bytes 1048592 | tf_op jit(solution)/shard_map/all_gather | solution.py:29
  163.2 2.5 gather_fusion.1
  165.7 76.2 %all-gather.21.cloned.1.call-done = bf16[32,1,256,128]{3,2,1,0:T(8,128)(2,1)} async-done(((bf16[1,1,256,128]{3,2,1,0:T(8,128)(2,1)}), bf16[32,1,256,128]{3,2,1,0:T(8,128)(2,1)}) %all-gather.21.cloned.1.call-update) | async-done | bytes 2097168 | tf_op jit(solution)/shard_map/all_gather | solution.py:28
  241.9 5.5 gather_fusion.2
  248.7 10.8 %scatter-add.26 = f32[7,128,640]{2,0,1:T(8,128)S(1)} dynamic-update-slice(f32[7,128,640]{2,0,1:T(8,128)S(1)} %fusion.67, f32[1,128,640]{2,0,1:T(1,128)} %get-tuple-element.156, s32[]{:T(128)} %constant.231.clone.1, s32[]{:T(128)} %constant.231.clone.1, s32[]{:T(128)} %constant.231.clone.1) | dynamic-update-slice | bytes 655364 | tf_op jit(solution)/shard_map/scatter-add | solution.py:101
  259.5 2.8 broadcast_select_fusion.10
  262.3 11.2 %scatter-add.29 = f32[7,128,640]{2,0,1:T(8,128)S(1)} dynamic-update-slice(f32[7,128,640]{2,0,1:T(8,128)S(1)} %scatter-add.26, f32[1,128,640]{2,0,1:T(1,128)} %broadcast_select_fusion.10, s32[]{:T(128)} %max.30, s32[]{:T(128)} %constant.231.clone.1, s32[]{:T(128)} %constant.231.clone.1) | dynamic-update-slice | bytes 655364 | tf_op jit(solution)/shard_map/scatter-add | solution.py:102
  276.0 5.5 fusion.28
  281.5 8.3 %bitcast_subtract_fusion.3 = f32[12,128,640]{2,1,0:T(8,128)S(1)} fusion(f32[12,128,640]{2,1,0:T(8,128)S(1)} %bitcast.227, f32[12,2,128,640]{3,0,2,1:T(8,128)S(1)} %fusion.28, f32[12,2,128]{2,1,0:T(2,128)S(1)} %copy.34, f32[12,128,128]{2,1,0:T(8,128)S(1)} %copy-done.12), kind=kOutput, calls=%fused_computation.33 | convolution fusion | flops 3021275136 | bytes 16527360 | tf_op jit(solution)/shard_map/tjrn,tjnc->trc/dot_general | solution.py:105
  289.8 8.2 %fusion.20 = f32[12,2,128,640]{3,2,1,0:T(8,128)S(1)} fusion(f32[12,128,640]{2,1,0:T(8,128)S(1)} %bitcast_subtract_fusion.3, f32[12,2,128]{2,1,0:T(2,128)S(1)} %copy.40, f32[12,128,128]{2,1,0:T(8,128)S(1)} %convert_select_fusion.2), kind=kOutput, calls=%fused_computation.28 | convolution fusion | flops 3020292096 | bytes 12595200 | tf_op jit(solution)/shard_map/tjrn,trc->tjnc/dot_general | solution.py:88
  298.0 8.1 %fusion.70 = f32[7,128,640]{2,0,1:T(8,128)S(1)} fusion(f32[12,2,128,640]{3,2,1,0:T(8,128)S(1)} %fusion.20, s32[12,2]{0,1:T(2,128)S(1)} %iota_add_fusion.3), kind=kOutput, calls=%fused_computation.64 | convolution fusion | flops 165150880 | bytes 10158176 | tf_op jit(solution)/shard_map/tjk,tjnc->knc/dot_general | solution.py:94
  306.5 7.6 %collective-permute-start.2 = (f32[1,128,640]{2,0,1:T(1,128)S(1)}, f32[1,128,640]{2,0,1:T(1,128)S(1)}, u32[]{:S(2)}, u32[]{:S(2)}) collective-permute-start(f32[1,128,640]{2,0,1:T(1,128)S(1)} %constant_dynamic-slice_fusion.7), channel_id=1, source_target_pairs={{0,32},{32,64},{64,96},{96,128},{128,160},{160,192},{192,224},{1,3... | collective-permute-start | bytes 983048 | tf_op jit(solution)/shard_map/ppermute | solution.py:17
  314.1 4.0 collective-permute-done.2
  321.5 2.5 gather_fusion.3
  324.0 71.8 %all-gather.25.cloned.1.call-done = bf16[32,1,256,128]{3,2,1,0:T(8,128)(2,1)} async-done(((bf16[1,1,256,128]{3,2,1,0:T(8,128)(2,1)}), bf16[32,1,256,128]{3,2,1,0:T(8,128)(2,1)}) %all-gather.25.cloned.1.call-update) | async-done | bytes 2097168 | tf_op jit(solution)/shard_map/all_gather | solution.py:28
  395.8 5.5 gather_fusion.4
  402.6 10.8 %scatter-add.30 = f32[7,128,640]{2,0,1:T(8,128)S(1)} dynamic-update-slice(f32[7,128,640]{2,0,1:T(8,128)S(1)} %fusion.70, f32[1,128,640]{2,0,1:T(1,128)} %get-tuple-element.154, s32[]{:T(128)} %constant.231.clone.1, s32[]{:T(128)} %constant.231.clone.1, s32[]{:T(128)} %constant.231.clone.1) | dynamic-update-slice | bytes 655364 | tf_op jit(solution)/shard_map/scatter-add | solution.py:101
  413.4 2.9 broadcast_select_fusion.7
  416.2 11.1 %scatter-add.31 = f32[7,128,640]{2,0,1:T(8,128)S(1)} dynamic-update-slice(f32[7,128,640]{2,0,1:T(8,128)S(1)} %scatter-add.30, f32[1,128,640]{2,0,1:T(1,128)} %broadcast_select_fusion.7, s32[]{:T(128)} %max.32, s32[]{:T(128)} %constant.231.clone.1, s32[]{:T(128)} %constant.231.clone.1) | dynamic-update-slice | bytes 655364 | tf_op jit(solution)/shard_map/scatter-add | solution.py:102
  429.9 5.5 fusion.26
  435.4 8.3 %bitcast_subtract_fusion.2 = f32[12,128,640]{2,1,0:T(8,128)S(1)} fusion(f32[12,128,640]{2,1,0:T(8,128)S(1)} %copy-done.5, f32[12,2,128,640]{3,0,2,1:T(8,128)S(1)} %fusion.26, f32[12,2,128]{2,1,0:T(2,128)S(1)} %copy.40, f32[12,128,128]{2,1,0:T(8,128)S(1)} %copy-done.10), kind=kOutput, calls=%fused_computation.32 | convolution fusion | flops 3021275136 | bytes 16527360 | tf_op jit(solution)/shard_map/tjrn,tjnc->trc/dot_general | solution.py:105
  443.7 8.2 %fusion.18 = f32[12,2,128,640]{3,2,1,0:T(8,128)S(1)} fusion(f32[12,128,640]{2,1,0:T(8,128)S(1)} %bitcast_subtract_fusion.2, f32[12,2,128]{2,1,0:T(2,128)S(1)} %copy.46, f32[12,128,128]{2,1,0:T(8,128)S(1)} %convert_select_fusion.1), kind=kOutput, calls=%fused_computation.26 | convolution fusion | flops 3020292096 | bytes 12595200 | tf_op jit(solution)/shard_map/tjrn,trc->tjnc/dot_general | solution.py:88
  451.9 8.1 %fusion.73 = f32[7,128,640]{2,0,1:T(8,128)S(1)} fusion(f32[12,2,128,640]{3,2,1,0:T(8,128)S(1)} %fusion.18, s32[12,2]{0,1:T(2,128)S(1)} %iota_add_fusion.2), kind=kOutput, calls=%fused_computation.65 | convolution fusion | flops 165150880 | bytes 10158176 | tf_op jit(solution)/shard_map/tjk,tjnc->knc/dot_general | solution.py:94
  460.4 7.6 %collective-permute-start.4 = (f32[1,128,640]{2,0,1:T(1,128)S(1)}, f32[1,128,640]{2,0,1:T(1,128)S(1)}, u32[]{:S(2)}, u32[]{:S(2)}) collective-permute-start(f32[1,128,640]{2,0,1:T(1,128)S(1)} %constant_dynamic-slice_fusion.4), channel_id=1, source_target_pairs={{0,32},{32,64},{64,96},{96,128},{128,160},{160,192},{192,224},{1,3... | collective-permute-start | bytes 983048 | tf_op jit(solution)/shard_map/ppermute | solution.py:17
  468.0 4.0 collective-permute-done.4
  475.4 2.5 gather_fusion.5
  477.9 71.9 %all-gather.29.cloned.1.call-done = bf16[32,1,256,128]{3,2,1,0:T(8,128)(2,1)} async-done(((bf16[1,1,256,128]{3,2,1,0:T(8,128)(2,1)}), bf16[32,1,256,128]{3,2,1,0:T(8,128)(2,1)}) %all-gather.29.cloned.1.call-update) | async-done | bytes 2097168 | tf_op jit(solution)/shard_map/all_gather | solution.py:28
  549.8 5.5 gather_fusion.6
  556.6 10.8 %scatter-add.34 = f32[7,128,640]{2,0,1:T(8,128)S(1)} dynamic-update-slice(f32[7,128,640]{2,0,1:T(8,128)S(1)} %fusion.73, f32[1,128,640]{2,0,1:T(1,128)} %get-tuple-element.152, s32[]{:T(128)} %constant.231.clone.1, s32[]{:T(128)} %constant.231.clone.1, s32[]{:T(128)} %constant.231.clone.1) | dynamic-update-slice | bytes 655364 | tf_op jit(solution)/shard_map/scatter-add | solution.py:101
  567.4 2.8 broadcast_select_fusion.4
  570.2 11.1 %scatter-add.35 = f32[7,128,640]{2,0,1:T(8,128)S(1)} dynamic-update-slice(f32[7,128,640]{2,0,1:T(8,128)S(1)} %scatter-add.34, f32[1,128,640]{2,0,1:T(1,128)} %broadcast_select_fusion.4, s32[]{:T(128)} %max.34, s32[]{:T(128)} %constant.231.clone.1, s32[]{:T(128)} %constant.231.clone.1) | dynamic-update-slice | bytes 655364 | tf_op jit(solution)/shard_map/scatter-add | solution.py:102
  583.8 5.5 fusion.24
  589.4 8.3 %bitcast_subtract_fusion.1 = f32[12,128,640]{2,1,0:T(8,128)S(1)} fusion(f32[12,128,640]{2,1,0:T(8,128)S(1)} %copy-done.3, f32[12,2,128,640]{3,0,2,1:T(8,128)S(1)} %fusion.24, f32[12,2,128]{2,1,0:T(2,128)S(1)} %copy.46, f32[12,128,128]{2,1,0:T(8,128)S(1)} %copy-done.8), kind=kOutput, calls=%fused_computation.31 | convolution fusion | flops 3021275136 | bytes 16527360 | tf_op jit(solution)/shard_map/tjrn,tjnc->trc/dot_general | solution.py:105
  597.7 8.2 %fusion.16 = f32[12,2,128,640]{3,2,1,0:T(8,128)S(1)} fusion(f32[12,128,640]{2,1,0:T(8,128)S(1)} %bitcast_subtract_fusion.1, f32[12,2,128]{2,1,0:T(2,128)S(1)} %copy.52, f32[12,128,128]{2,1,0:T(8,128)S(1)} %convert_select_fusion), kind=kOutput, calls=%fused_computation.24 | convolution fusion | flops 3020292096 | bytes 12595200 | tf_op jit(solution)/shard_map/tjrn,trc->tjnc/dot_general | solution.py:88
  605.9 8.1 %fusion.76 = f32[7,128,640]{2,0,1:T(8,128)S(1)} fusion(f32[12,2,128,640]{3,2,1,0:T(8,128)S(1)} %fusion.16, s32[12,2]{0,1:T(2,128)S(1)} %iota_add_fusion.1), kind=kOutput, calls=%fused_computation.66 | convolution fusion | flops 165150880 | bytes 10158176 | tf_op jit(solution)/shard_map/tjk,tjnc->knc/dot_general | solution.py:94
  615.0 7.5 %collective-permute-start.6 = (f32[1,128,640]{2,0,1:T(1,128)}, f32[1,128,640]{2,0,1:T(1,128)}, u32[]{:S(2)}, u32[]{:S(2)}) collective-permute-start(f32[1,128,640]{2,0,1:T(1,128)} %constant_dynamic-slice_fusion.1), channel_id=1, source_target_pairs={{0,32},{32,64},{64,96},{96,128},{128,160},{160,192},{192,224},{1,3... | collective-permute-start | bytes 983048 | tf_op jit(solution)/shard_map/ppermute | solution.py:17
  631.3 2.5 gather_fusion.7
  633.8 10.7 %scatter-add.36 = f32[7,128,640]{2,0,1:T(8,128)S(1)} dynamic-update-slice(f32[7,128,640]{2,0,1:T(8,128)S(1)} %fusion.76, f32[1,128,640]{2,0,1:T(1,128)} %get-tuple-element.150, s32[]{:T(128)} %constant.231.clone.1, s32[]{:T(128)} %constant.231.clone.1, s32[]{:T(128)} %constant.231.clone.1) | dynamic-update-slice | bytes 655364 | tf_op jit(solution)/shard_map/scatter-add | solution.py:101
  644.5 2.8 broadcast_select_fusion.1
  647.3 11.0 %scatter-add.39 = f32[7,128,640]{2,0,1:T(8,128)S(1)} dynamic-update-slice(f32[7,128,640]{2,0,1:T(8,128)S(1)} %scatter-add.36, f32[1,128,640]{2,0,1:T(1,128)} %broadcast_select_fusion.1, s32[]{:T(128)} %max.36, s32[]{:T(128)} %constant.231.clone.1, s32[]{:T(128)} %constant.231.clone.1) | dynamic-update-slice | bytes 655364 | tf_op jit(solution)/shard_map/scatter-add | solution.py:102
  660.8 5.5 fusion.22
  666.3 9.6 %bitcast_subtract_fusion = f32[12,128,640]{2,1,0:T(8,128)} fusion(f32[12,128,640]{2,1,0:T(8,128)S(1)} %copy-done.1, f32[12,2,128,640]{3,0,2,1:T(8,128)S(1)} %fusion.22, f32[12,2,128]{2,1,0:T(2,128)S(1)} %copy.52, f32[12,128,128]{2,1,0:T(8,128)S(1)} %convert_select_fusion), kind=kOutput, calls=%fused_computation.30 | convolution fusion | flops 3021275136 | bytes 16527360 | tf_op jit(solution)/shard_map/tjrn,tjnc->trc/dot_general | solution.py:105
  (126 shorter events, 56.3 us)
Async XLA Ops:
  6.5 81.2 %all-gather.17.cloned.1.call-start = ((), (), s32[]{:S(2)}) async-start(), calls=%async_computation | async-start | bytes 2162688 | tf_op jit(solution)/shard_map/all_gather | solution.py:28
  8.2 155.1 %all-gather.19.cloned.1.call-start = ((), (), s32[]{:S(2)}) async-start(), calls=%async_computation.1 | async-start | bytes 1081344 | tf_op jit(solution)/shard_map/all_gather | solution.py:29
  9.7 232.2 %all-gather.21.cloned.1.call-start = ((), (), s32[]{:S(2)}) async-start(), calls=%async_computation.2 | async-start | bytes 2162688 | tf_op jit(solution)/shard_map/all_gather | solution.py:28
  10.5 311.0 %all-gather.23.cloned.1.call-start = ((), (), s32[]{:S(2)}) async-start(), calls=%async_computation.3 | async-start | bytes 1081344 | tf_op jit(solution)/shard_map/all_gather | solution.py:29
  11.0 384.7 %all-gather.25.cloned.1.call-start = ((), (), s32[]{:S(2)}) async-start(), calls=%async_computation.4 | async-start | bytes 2162688 | tf_op jit(solution)/shard_map/all_gather | solution.py:28
  11.6 463.7 %all-gather.27.cloned.1.call-start = ((), (), s32[]{:S(2)}) async-start(), calls=%async_computation.5 | async-start | bytes 1081344 | tf_op jit(solution)/shard_map/all_gather | solution.py:29
  12.2 537.6 %all-gather.29.cloned.1.call-start = ((), (), s32[]{:S(2)}) async-start(), calls=%async_computation.6 | async-start | bytes 2162688 | tf_op jit(solution)/shard_map/all_gather | solution.py:28
  13.0 618.3 %all-gather.31.cloned.1.call-start = ((), (), s32[]{:S(2)}) async-start(), calls=%async_computation.7 | async-start | bytes 1081344 | tf_op jit(solution)/shard_map/all_gather | solution.py:29
  92.8 0.9 copy-start.11
  112.4 11.6 %collective-permute-start = (f32[1,128,640]{2,0,1:T(1,128)S(1)}, f32[1,128,640]{2,0,1:T(1,128)S(1)}, u32[]{:S(2)}, u32[]{:S(2)}) collective-permute-start(f32[1,128,640]{2,0,1:T(1,128)S(1)} %constant_dynamic-slice_fusion.10), channel_id=1, source_target_pairs={{0,32},{32,64},{64,96},{96,128},{128,160},{160,192},{192,224},{1,3... | collective-permute-start | bytes 983048 | tf_op jit(solution)/shard_map/ppermute | solution.py:17
  125.4 134.1 %collective-permute-start.1 = (f32[1,128,640]{2,0,1:T(1,128)}, f32[1,128,640]{2,0,1:T(1,128)}, u32[]{:S(2)}, u32[]{:S(2)}) collective-permute-start(f32[1,128,640]{2,0,1:T(1,128)} %get-tuple-element.155), channel_id=1, source_target_pairs={{32,0},{64,32},{96,64},{128,96},{160,128},{192,160},{224,192},{33,... | collective-permute-start | bytes 983048 | tf_op jit(solution)/shard_map/ppermute | solution.py:19
  248.7 41.1 %copy-start.9 = (f32[12,128,128]{2,1,0:T(8,128)}, f32[12,128,128]{2,1,0:T(8,128)S(1)}, u32[]{:S(2)}) copy-start(f32[12,128,128]{2,1,0:T(8,128)S(1)} %convert_select_fusion.2) | copy-start | bytes 2359300
  275.9 5.5 copy-start.6
  276.0 5.5 copy-start.12
  289.8 8.2 %copy-start.4 = (f32[12,128,640]{2,1,0:T(8,128)}, f32[12,128,640]{2,1,0:T(8,128)S(1)}, u32[]{:S(2)}) copy-start(f32[12,128,640]{2,1,0:T(8,128)S(1)} %bitcast_subtract_fusion.3) | copy-start | bytes 11796484
  306.5 11.6 %collective-permute-start.2 = (f32[1,128,640]{2,0,1:T(1,128)S(1)}, f32[1,128,640]{2,0,1:T(1,128)S(1)}, u32[]{:S(2)}, u32[]{:S(2)}) collective-permute-start(f32[1,128,640]{2,0,1:T(1,128)S(1)} %constant_dynamic-slice_fusion.7), channel_id=1, source_target_pairs={{0,32},{32,64},{64,96},{96,128},{128,160},{160,192},{192,224},{1,3... | collective-permute-start | bytes 983048 | tf_op jit(solution)/shard_map/ppermute | solution.py:17
  319.5 93.8 %collective-permute-start.3 = (f32[1,128,640]{2,0,1:T(1,128)}, f32[1,128,640]{2,0,1:T(1,128)}, u32[]{:S(2)}, u32[]{:S(2)}) collective-permute-start(f32[1,128,640]{2,0,1:T(1,128)} %get-tuple-element.153), channel_id=1, source_target_pairs={{32,0},{64,32},{96,64},{128,96},{160,128},{192,160},{224,192},{33,... | collective-permute-start | bytes 983048 | tf_op jit(solution)/shard_map/ppermute | solution.py:19
  402.5 41.1 %copy-start.7 = (f32[12,128,128]{2,1,0:T(8,128)}, f32[12,128,128]{2,1,0:T(8,128)S(1)}, u32[]{:S(2)}) copy-start(f32[12,128,128]{2,1,0:T(8,128)S(1)} %convert_select_fusion.1) | copy-start | bytes 2359300
  429.8 5.5 copy-start.5
  429.8 5.5 copy-start.10
  443.7 8.2 %copy-start.2 = (f32[12,128,640]{2,1,0:T(8,128)}, f32[12,128,640]{2,1,0:T(8,128)S(1)}, u32[]{:S(2)}) copy-start(f32[12,128,640]{2,1,0:T(8,128)S(1)} %bitcast_subtract_fusion.2) | copy-start | bytes 11796484
  460.4 11.6 %collective-permute-start.4 = (f32[1,128,640]{2,0,1:T(1,128)S(1)}, f32[1,128,640]{2,0,1:T(1,128)S(1)}, u32[]{:S(2)}, u32[]{:S(2)}) collective-permute-start(f32[1,128,640]{2,0,1:T(1,128)S(1)} %constant_dynamic-slice_fusion.4), channel_id=1, source_target_pairs={{0,32},{32,64},{64,96},{96,128},{128,160},{160,192},{192,224},{1,3... | collective-permute-start | bytes 983048 | tf_op jit(solution)/shard_map/ppermute | solution.py:17
  473.4 93.9 %collective-permute-start.5 = (f32[1,128,640]{2,0,1:T(1,128)}, f32[1,128,640]{2,0,1:T(1,128)}, u32[]{:S(2)}, u32[]{:S(2)}) collective-permute-start(f32[1,128,640]{2,0,1:T(1,128)} %get-tuple-element.151), channel_id=1, source_target_pairs={{32,0},{64,32},{96,64},{128,96},{160,128},{192,160},{224,192},{33,... | collective-permute-start | bytes 983048 | tf_op jit(solution)/shard_map/ppermute | solution.py:19
  583.8 5.5 copy-start.3
  583.8 5.5 copy-start.8
  597.7 8.2 %copy-start = (f32[12,128,640]{2,1,0:T(8,128)}, f32[12,128,640]{2,1,0:T(8,128)S(1)}, u32[]{:S(2)}) copy-start(f32[12,128,640]{2,1,0:T(8,128)S(1)} %bitcast_subtract_fusion.1) | copy-start | bytes 11796484
  615.0 11.9 %collective-permute-start.6 = (f32[1,128,640]{2,0,1:T(1,128)}, f32[1,128,640]{2,0,1:T(1,128)}, u32[]{:S(2)}, u32[]{:S(2)}) collective-permute-start(f32[1,128,640]{2,0,1:T(1,128)} %constant_dynamic-slice_fusion.1), channel_id=1, source_target_pairs={{0,32},{32,64},{64,96},{96,128},{128,160},{160,192},{192,224},{1,3... | collective-permute-start | bytes 983048 | tf_op jit(solution)/shard_map/ppermute | solution.py:17
  629.3 15.2 %collective-permute-start.7 = (f32[1,128,640]{2,0,1:T(1,128)}, f32[1,128,640]{2,0,1:T(1,128)}, u32[]{:S(2)}, u32[]{:S(2)}) collective-permute-start(f32[1,128,640]{2,0,1:T(1,128)} %get-tuple-element.149), channel_id=1, source_target_pairs={{32,0},{64,32},{96,64},{128,96},{160,128},{192,160},{224,192},{33,... | collective-permute-start | bytes 983048 | tf_op jit(solution)/shard_map/ppermute | solution.py:19
  660.8 5.5 copy-start.1
Sparse Core Ops, SparseCore 0:
  9.9 77.7 all-gather.16
  90.4 72.8 all-gather.18
  165.8 76.0 all-gather.20
  244.4 72.8 all-gather.22
  319.7 76.0 all-gather.24
  398.2 72.8 all-gather.26
  473.7 76.0 all-gather.28
  552.3 72.8 all-gather.30
where the time goes:
time: 689 us; the launch traced here: 683 us
  waiting for transfers between devices  319 us (46%)
  matrix products  134 us (19%)
  local copies, waits for them, and re-layouts  127 us (18%)
  starting transfers between devices  38.2 us (6%)
  other arithmetic  35.4 us (5%)
  between operations  30.1 us (4%)
    all_gather x4, waiting for transfers between devices, fetch_blocks(): lax.all_gather(local_refl, 'col', axis=0, tiled=True)  265 us
    scatter-add x4, local copies, waits for them, and re-layouts, on_device(): inner_sums.at[last_slot].add(jnp.where(from_after, padded[3], 0.0))  44.5 us
    scatter-add x4, local copies, waits for them, and re-layouts, on_device(): inner_sums = inner_sums.at[0].add(jnp.where(from_before, padded[0], 0.0))  43.1 us
    all_gather x4, waiting for transfers between devices, fetch_blocks(): lax.all_gather(local_factor, 'col', axis=0, tiled=True)  36 us
    dot_general x4, matrix products, on_device(): jnp.einsum('tjrn,trc->tjnc', reflector_tiles, slab_tiles, precision=highest)  34.9 us
    dot_general x4, matrix products, on_device(): jnp.einsum('tjrn,tjnc->trc', reflector_tiles, spread, precision=highest)  34.5 us
    dot_general x4, matrix products, on_device(): jnp.einsum('tjk,tjnc->knc', selector, partial_value, precision=highest)  32.6 us
    ppermute x4, starting transfers between devices, with_halo(): lax.ppermute(tail, axis, [(i, (i + 1) % count) for i in range(ends)])  30.2 us
  transfers between devices with their start and end apart: 16, of which 9 were waited for; matrix products, arithmetic and copies ran while one was open for 38% of the time, Pallas kernels for 0%

commit v1 on v0

v1 whole, which is shorter than its diff:
```python
import functools

import jax
import jax.numpy as jnp
from jax import lax
from jax.experimental import pallas as pl
from jax.experimental.pallas import tpu as pltpu
from jax.sharding import PartitionSpec as P

SWEEPS = 4
LEN = 256
NB = 128
SLOTS = 7
TILES = 6
ZX = 4
BLK = LEN + NB
MESH = pl.DeviceIdType.MESH
F32 = jnp.float32
BF16 = jnp.bfloat16


def split(value):
    high = value.astype(BF16)
    low = (value - high.astype(F32)).astype(BF16)
    return high, low


def dot(left, right):
    return jnp.dot(left, right, preferred_element_type=F32)


def kernel(nx, nz, nrow, tab, slab, refl, fact, out, x, own, pieces, blocks, vt, wbuf, wrec,
           load_sem, store_sem, a2a_sem, zx_send, zx_recv, xs_send, xs_recv, xz_send, xz_recv, zs_send, zs_recv,
           w_send, w_recv):
    ncol = nx * nz
    me = lax.axis_index("col")
    row = lax.axis_index("row")
    mx, mz = me // nz, me % nz
    piece = BLK // nz
    cols = x.shape[1]
    loads = pltpu.make_async_copy(slab, x, load_sem)
    loads.start()

    right_row, left_row = (row + 1) % nrow, (row + nrow - 1) % nrow
    barrier = pltpu.get_barrier_semaphore()

    def greet(k, carry):
        pl.semaphore_signal(barrier, inc=1, device_id={"col": (me + k) % ncol}, device_id_type=MESH)
        return carry

    lax.fori_loop(1, ncol, greet, 0)
    pl.semaphore_signal(barrier, inc=1, device_id={"row": right_row}, device_id_type=MESH)
    pl.semaphore_signal(barrier, inc=1, device_id={"row": left_row}, device_id_type=MESH)

    ri = lax.broadcasted_iota(jnp.int32, (LEN, LEN), 0)
    ci = lax.broadcasted_iota(jnp.int32, (LEN, LEN), 1)
    for s in range(SWEEPS):
        place = (((ri - tab[s, 24]) & (LEN - 1)) == ci).astype(BF16)
        own[s, pl.ds(0, LEN), :] = dot(place, refl[s, 0]).astype(BF16)
        own[s, pl.ds(LEN, NB), :] = fact[s, 0]

    pl.semaphore_wait(barrier, ncol + 1)

    def send_piece(k, carry):
        to = (me + k) % ncol
        pltpu.make_async_remote_copy(
            src_ref=own.at[to // nz, pl.ds(pl.multiple_of((to % nz) * piece, 16), piece), :],
            dst_ref=pieces.at[me],
            send_sem=a2a_sem.at[0],
            recv_sem=a2a_sem.at[1],
            device_id={"col": to},
            device_id_type=MESH,
        ).start()
        return carry

    lax.fori_loop(1, ncol, send_piece, 0)
    my_rows = pl.ds(pl.multiple_of(mz * piece, 16), piece)
    pieces[me] = own[mx, my_rows, :]
    everything = pieces.at[pl.ds(0, ncol - 1)]
    pltpu.make_async_copy(everything, everything, a2a_sem.at[1]).wait()
    for t in range(SLOTS):
        found = pieces[tab[mx, 8 + t]].astype(F32) * tab[mx, 16 + t].astype(F32)
        blocks[mx, t, my_rows, :] = found.astype(BF16)
    pltpu.make_async_copy(everything, everything, a2a_sem.at[0]).wait()

    def col_of(cx, cz):
        return ((cx + nx) % nx) * nz + (cz + nz) % nz

    def rows_of(cz):
        return pl.ds(pl.multiple_of(((cz + nz) % nz) * piece, 16), piece)

    def move(part, to, send, recv):
        copy = pltpu.make_async_remote_copy(
            src_ref=part, dst_ref=part, send_sem=send, recv_sem=recv, device_id={"col": to}, device_id_type=MESH)
        copy.start()
        return copy

    first = pl.ds(0, ZX)
    second = pl.ds(ZX, SLOTS - ZX)
    n_cw, n_ccw = nz // 2, (nz - 1) // 2
    sent = []

    def zx_step(k, way):
        part = blocks.at[mx, first, rows_of(mz - way * k), :]
        i = k if way > 0 else n_cw + k
        copy = move(part, col_of(mx, mz + way), zx_send.at[i], zx_recv.at[i])
        sent.append(copy)
        return copy

    def zs_step(k, way):
        part = blocks.at[:, second, rows_of(mz - way * k), :]
        i = k if way > 0 else n_cw + k
        copy = move(part, col_of(mx, mz + way), zs_send.at[i], zs_recv.at[i])
        sent.append(copy)
        return copy

    mine = blocks.at[mx, second, my_rows, :]
    xz = [move(mine, col_of(mx + k, mz), xz_send.at[k - 1], xz_recv.at[k - 1]) for k in range(1, nx)]
    sent.extend(xz)
    cw = zx_step(0, 1)
    ccw = zx_step(0, -1) if n_ccw else None
    for copy in xz:
        copy.wait_recv()
    zcw = zs_step(0, 1)
    zccw = zs_step(0, -1) if n_ccw else None
    for k in range(n_cw):
        cw.wait_recv()
        if k + 1 < n_cw:
            cw = zx_step(k + 1, 1)
        if k < n_ccw:
            ccw.wait_recv()
            if k + 1 < n_ccw:
                ccw = zx_step(k + 1, -1)
    xs = [
        move(blocks.at[mx, first], col_of(mx + way, mz), xs_send.at[i], xs_recv.at[i])
        for i, way in enumerate((1, -1))
    ]
    sent.extend(xs)
    half = ZX // 2
    far = []
    for k in range(n_cw):
        zcw.wait_recv()
        if k + 1 < n_cw:
            zcw = zs_step(k + 1, 1)
        if k < n_ccw:
            zccw.wait_recv()
            if k + 1 < n_ccw:
                zccw = zs_step(k + 1, -1)
        if k == n_cw // 2:
            for i, way in enumerate((1, -1)):
                xs[i].wait_recv()
                part = blocks.at[(mx - way + nx) % nx, pl.ds(i * half, half)]
                far.append(move(part, col_of(mx + way, mz), xs_send.at[2 + i], xs_recv.at[2 + i]))
    sent.extend(far)
    for copy in far:
        copy.wait_recv()
    for copy in sent:
        copy.wait_send()
    loads.wait()

    at = lax.broadcasted_iota(jnp.int32, (LEN, 1), 0)

    def inner(v_t, z):
        high, low = split(z)
        return dot(v_t, high) + dot(v_t, low)

    def change(s, t, w):
        f = blocks[s, t, pl.ds(LEN, NB), :]
        v = blocks[s, t, pl.ds(0, LEN), :]
        y = dot(jnp.concatenate([f, f], axis=1), jnp.concatenate(split(w), axis=0))
        return dot(jnp.concatenate([v, v], axis=1), jnp.concatenate(split(y), axis=0))

    def tile(t):
        return pl.ds(pl.multiple_of(t * LEN, LEN), LEN)

    last = pl.ds((TILES - 1) * LEN, LEN)

    def sweep(s, carry):
        for t in range(SLOTS):
            vt[t] = blocks[s, t, pl.ds(0, LEN), :].T
        d_first, d_last = tab[s, 0], tab[s, SLOTS - 1]
        wbuf[0] = inner(vt[0], jnp.where(at < d_first, x[pl.ds(0, LEN), :], 0.0))
        wbuf[1] = inner(vt[SLOTS - 1], jnp.where(at >= d_last, x[last, :], 0.0))
        par = s % 2
        copies = [
            pltpu.make_async_remote_copy(
                src_ref=wbuf.at[side], dst_ref=wrec.at[par, 1 - side], send_sem=w_send.at[side],
                recv_sem=w_recv.at[par, 1 - side], device_id={"row": to}, device_id_type=MESH)
            for side, to in ((0, left_row), (1, right_row))
        ]
        for copy in copies:
            copy.start()

        def body(t, carry):
            d = tab[s, t + 1]
            z = jnp.where(at >= d, x[tile(t), :], x[tile(t + 1), :])
            delta = change(s, t + 1, inner(vt[t + 1], z))
            x[tile(t), :] = x[tile(t), :] - jnp.where(at >= d, delta, 0.0)
            x[tile(t + 1), :] = x[tile(t + 1), :] - jnp.where(at < d, delta, 0.0)
            return carry

        lax.fori_loop(0, TILES - 1, body, 0)
        for copy in copies:
            copy.wait()
        delta = change(s, 0, wbuf[0] + wrec[par, 0])
        x[pl.ds(0, LEN), :] = x[pl.ds(0, LEN), :] - jnp.where(at < d_first, delta, 0.0)
        delta = change(s, SLOTS - 1, wbuf[1] + wrec[par, 1])
        x[last, :] = x[last, :] - jnp.where(at >= d_last, delta, 0.0)
        return carry

    lax.fori_loop(0, SWEEPS, sweep, 0)
    stores = pltpu.make_async_copy(x, out, store_sem)
    stores.start()
    stores.wait()


def tables(offsets, owners):
    row, col = lax.axis_index("row"), lax.axis_index("col")
    begin_tile = offsets // LEN
    within = offsets % LEN
    slot = jnp.arange(8, dtype=jnp.int32) + (row * TILES - 1)
    slot = jnp.where(jnp.arange(8) < SLOTS, slot, -2)
    match = (begin_tile[:, None, :] == slot[None, :, None]).astype(jnp.int32)
    own = jnp.sum((owners == col) * within, axis=1, keepdims=True)
    return jnp.concatenate(
        [
            jnp.sum(match * within[:, None, :], axis=2),
            jnp.sum(match * owners[:, None, :], axis=2),
            jnp.sum(match, axis=2),
            jnp.broadcast_to(own, (SWEEPS, 8)),
        ],
        axis=1,
    ).astype(jnp.int32)


def on_device(nx, nz, nrow, slab, reflectors, factors, offsets, owners):
    cols = slab.shape[1]
    ncol = nx * nz
    dma = pltpu.SemaphoreType.DMA
    n_ring = nz - 1
    return pl.pallas_call(
        functools.partial(kernel, nx, nz, nrow),
        out_shape=jax.ShapeDtypeStruct(slab.shape, F32),
        in_specs=[
            pl.BlockSpec(memory_space=pltpu.SMEM),
            pl.BlockSpec(memory_space=pl.ANY),
            pl.BlockSpec(memory_space=pltpu.VMEM),
            pl.BlockSpec(memory_space=pltpu.VMEM),
        ],
        out_specs=pl.BlockSpec(memory_space=pl.ANY),
        scratch_shapes=[
            pltpu.VMEM(slab.shape, F32),
            pltpu.VMEM((SWEEPS, BLK, NB), BF16),
            pltpu.VMEM((ncol, BLK // nz, NB), BF16),
            pltpu.VMEM((nx, SLOTS, BLK, NB), BF16),
            pltpu.VMEM((SLOTS, NB, LEN), BF16),
            pltpu.VMEM((2, NB, cols), F32),
            pltpu.VMEM((2, 2, NB, cols), F32),
            dma, dma, dma((2,)),
            dma((n_ring,)), dma((n_ring,)),
            dma((4,)), dma((4,)),
            dma((nx - 1,)), dma((nx - 1,)),
            dma((n_ring,)), dma((n_ring,)),
            dma((2,)), dma((2, 2)),
        ],
        compiler_params=pltpu.CompilerParams(
            collective_id=0, has_side_effects=True, vmem_limit_bytes=56 * 2**20
        ),
        cost_estimate=pl.CostEstimate(flops=6_000_000_000, bytes_accessed=9_000_000, transcendentals=0),
    )(tables(offsets, owners), slab, reflectors, factors)


def solution(mesh):
    nx = SWEEPS
    nz = mesh.shape["col"] // nx
    placed = (P("row", "col"), P(None, "col", None, None), P(None, "col", None, None), P(), P())
    return jax.shard_map(
        functools.partial(on_device, nx, nz, mesh.shape["row"]),
        mesh=mesh, in_specs=placed, out_specs=P("row", "col"), check_vma=False,
    )
```

time: 689 us -> 92.6 us (0.13)
  waiting for transfers between devices: 319 us -> 0 us
  matrix products: 134 us -> 0 us
  local copies, waits for them, and re-layouts: 127 us -> 4.36 us
  Pallas kernels: 0 us -> 84.2 us
  starting transfers between devices: 38.2 us -> 0 us
  other arithmetic: 35.4 us -> 2.51 us
  between operations: 30.1 us -> 0.01 us
    all_gather x8 -> x0, waiting for transfers between devices: 301 us -> none  [the longest x4 265 us: fetch_blocks(): lax.all_gather(local_refl, 'col', axis=0, tiled=True)]
    dot_general x20 -> x0, matrix products: 134 us -> none  [the longest x4 34.9 us: on_device(): jnp.einsum('tjrn,trc->tjnc', reflector_tiles, slab_tiles, precision=highest)]
    scatter-add x8 -> x0, local copies, waits for them, and re-layouts: 87.5 us -> none  [the longest x4 44.5 us: on_device(): inner_sums.at[last_slot].add(jnp.where(from_after, padded[3], 0.0))]
    pallas_call x0 -> x1, Pallas kernels: none -> 84.2 us  [on_device(): pl.pallas_call(functools.partial(kernel, nx, nz, nrow), out_shape=jax.Sha...]
    ppermute x8 -> x0, starting transfers between devices: 37.9 us -> none  [the longest x4 30.2 us: with_halo(): lax.ppermute(tail, axis, [(i, (i + 1) % count) for i in range(ends)])]
    gather x8 -> x0, local copies, waits for them, and re-layouts: 31.2 us -> none  [the longest x4 21.3 us: on_device(): flat_rows[holders * span_rows + position].astype(jnp.float32)]
    another operation x9 -> x0, other arithmetic: 19.5 us -> none
    ppermute x8 -> x0, waiting for transfers between devices: 14.4 us -> none  [the longest x4 14.4 us: with_halo(): lax.ppermute(tail, axis, [(i, (i + 1) % count) for i in range(ends)])]
  transfers between devices with their start and end apart: 16 -> 0, of which waited for: 9 -> 0; matrix products, arithmetic and copies ran while one was open for 38% -> 0% of each run, Pallas kernels for 0% -> 0%
where the time goes in v1:
time: 92.6 us; the launch traced here: 91 us
  Pallas kernels  84.2 us (91%)
  local copies, waits for them, and re-layouts  4.36 us (5%)
  other arithmetic  2.51 us (3%)
    pallas_call x1, Pallas kernels, on_device(): pl.pallas_call(functools.partial(kernel, nx, nz, nrow), out_shape=jax.Sha...  84.2 us
    unnamed x1, local copies, waits for them, and re-layouts  4.29 us

profile of v1, /device:TPU:1, one launch (start us, length us, event | category | flops | bytes accessed | tf_op | source)
XLA Modules:
  0.0 91.0 jit_solution(13992900682749842160)
XLA Ops:
  0.0 0.8 add_select_fusion.1
  0.8 1.0 %fusion = (s32[4,8]{1,0:T(4,128)S(1)}, s32[4,8]{1,0:T(4,128)S(1)}, s32[4,8]{1,0:T(4,128)S(1)}) fusion(s32[4,32]{1,0:T(4,128)S(1)} %get-tuple-element.10, s32[4,32]{1,0:T(4,128)S(1)} %get-tuple-element.8, s32[8]{0:T(128)S(1)} %compare_select_fusion.2, s32[4,32]{1,0:T(4,128)} %param.9), kind=kLoop, calls=%fused_computation.3 | loop fusion | flops 7072 | bytes 1952 | tf_op jit(solution)/shard_map/reduce_sum | solution.py:227
  1.9 0.1 broadcast_in_dim.7
  1.9 0.7 pad_add_fusion.tab
  2.6 84.2 %shard_map.55 = f32[1536,640]{1,0:T(8,128)} custom-call(s32[4,32]{1,0:T(4,128)} %pad_add_fusion.tab, f32[1536,640]{1,0:T(8,128)} %slab.1, bf16[4,1,256,128]{3,2,1,0:T(8,128)(2,1)} %refl.1, bf16[4,1,128,128]{3,2,1,0:T(8,128)(2,1)} %fact.1), custom_call_target="tpu_custom_call" | custom-call | flops 6000000000 | bytes 9000000 | tf_op jit(solution)/shard_map/pallas_call | solution.py:241
  86.8 4.3 %copy.7 = f32[1536,640]{1,0:T(8,128)} copy(f32[1536,640]{1,0:T(8,128)} %shard_map.55) | data formatting | bytes 7864320
  (1 shorter events, 0.0 us)

commit v2 on v1

--- a/solution.py
+++ b/solution.py
@@ -29,8 +29,8 @@
     return jnp.dot(left, right, preferred_element_type=F32)
 
 
-def kernel(nx, nz, nrow, tab, slab, refl, fact, out, x, own, pieces, blocks, vt, wbuf, wrec,
-           load_sem, store_sem, a2a_sem, zx_send, zx_recv, xs_send, xs_recv, xz_send, xz_recv, zs_send, zs_recv,
+def kernel(nx, nz, nrow, cut, tab, slab, refl, fact, x, own, pieces, blocks, vt, vpair, ys, wbuf, wrec,
+           load_sem, a2a_sem, zx_send, zx_recv, xs_send, xs_recv, xz_send, xz_recv, zs_send, zs_recv,
            w_send, w_recv):
     ncol = nx * nz
     me = lax.axis_index("col")
@@ -159,59 +159,80 @@
     loads.wait()
 
     at = lax.broadcasted_iota(jnp.int32, (LEN, 1), 0)
-
-    def inner(v_t, z):
+    halves = [(0, cut), (cut, cols - cut)] if cut < cols else [(0, cols)]
+
+    def keep(value, mask):
+        return jnp.where(mask, value.astype(F32), 0.0).astype(BF16)
+
+    def tile(t, h):
+        return x[pl.ds(t * LEN, LEN), pl.ds(*halves[h])]
+
+    def inner(s, t, h):
+        d = tab[s, t]
+        if t == 0:
+            z = jnp.where(at < d, tile(0, h), 0.0)
+        elif t == SLOTS - 1:
+            z = jnp.where(at >= d, tile(TILES - 1, h), 0.0)
+        else:
+            z = jnp.where(at >= d, tile(t - 1, h), tile(t, h))
         high, low = split(z)
-        return dot(v_t, high) + dot(v_t, low)
-
-    def change(s, t, w):
+        return dot(vt[t], high) + dot(vt[t], low)
+
+    def scale(s, t, h, w):
         f = blocks[s, t, pl.ds(LEN, NB), :]
-        v = blocks[s, t, pl.ds(0, LEN), :]
         y = dot(jnp.concatenate([f, f], axis=1), jnp.concatenate(split(w), axis=0))
-        return dot(jnp.concatenate([v, v], axis=1), jnp.concatenate(split(y), axis=0))
-
-    def tile(t):
-        return pl.ds(pl.multiple_of(t * LEN, LEN), LEN)
-
-    last = pl.ds((TILES - 1) * LEN, LEN)
+        ys[t, :, pl.ds(*halves[h])] = jnp.concatenate(split(y), axis=0)
+
+    def apply(s, t, h):
+        here = pl.ds(t * LEN, LEN), pl.ds(*halves[h])
+        delta = dot(vpair[t], ys[pl.ds(t, 2), :, pl.ds(*halves[h])].reshape(4 * NB, halves[h][1]))
+        x[here] = x[here] - delta
+
+    def exchange(s, h):
+        par = s % 2
+        part = pl.ds(*halves[h])
+        return [
+            pltpu.make_async_remote_copy(
+                src_ref=wbuf.at[par, side, :, part], dst_ref=wrec.at[par, 1 - side, :, part],
+                send_sem=w_send.at[par, side, h], recv_sem=w_recv.at[par, 1 - side, h],
+                device_id={"row": to}, device_id_type=MESH)
+            for side, to in ((0, left_row), (1, right_row))
+        ]
+
+    def edges(s, h):
+        wbuf[s % 2, 0, :, pl.ds(*halves[h])] = inner(s, 0, h)
+        wbuf[s % 2, 1, :, pl.ds(*halves[h])] = inner(s, SLOTS - 1, h)
+        for copy in exchange(s, h):
+            copy.start()
+
+    def finish(s, h):
+        for copy in exchange(s, h):
+            copy.wait()
+        part = pl.ds(*halves[h])
+        for side, t in ((0, 0), (1, SLOTS - 1)):
+            scale(s, t, h, wbuf[s % 2, side, :, part] + wrec[s % 2, side, :, part])
+        apply(s, 0, h)
+        apply(s, TILES - 1, h)
 
     def sweep(s, carry):
         for t in range(SLOTS):
             vt[t] = blocks[s, t, pl.ds(0, LEN), :].T
-        d_first, d_last = tab[s, 0], tab[s, SLOTS - 1]
-        wbuf[0] = inner(vt[0], jnp.where(at < d_first, x[pl.ds(0, LEN), :], 0.0))
-        wbuf[1] = inner(vt[SLOTS - 1], jnp.where(at >= d_last, x[last, :], 0.0))
-        par = s % 2
-        copies = [
-            pltpu.make_async_remote_copy(
-                src_ref=wbuf.at[side], dst_ref=wrec.at[par, 1 - side], send_sem=w_send.at[side],
-                recv_sem=w_recv.at[par, 1 - side], device_id={"row": to}, device_id_type=MESH)
-            for side, to in ((0, left_row), (1, right_row))
-        ]
-        for copy in copies:
-            copy.start()
-
-        def body(t, carry):
-            d = tab[s, t + 1]
-            z = jnp.where(at >= d, x[tile(t), :], x[tile(t + 1), :])
-            delta = change(s, t + 1, inner(vt[t + 1], z))
-            x[tile(t), :] = x[tile(t), :] - jnp.where(at >= d, delta, 0.0)
-            x[tile(t + 1), :] = x[tile(t + 1), :] - jnp.where(at < d, delta, 0.0)
-            return carry
-
-        lax.fori_loop(0, TILES - 1, body, 0)
-        for copy in copies:
-            copy.wait()
-        delta = change(s, 0, wbuf[0] + wrec[par, 0])
-        x[pl.ds(0, LEN), :] = x[pl.ds(0, LEN), :] - jnp.where(at < d_first, delta, 0.0)
-        delta = change(s, SLOTS - 1, wbuf[1] + wrec[par, 1])
-        x[last, :] = x[last, :] - jnp.where(at >= d_last, delta, 0.0)
+        for h in range(len(halves)):
+            edges(s, h)
+            for t in range(1, SLOTS - 1):
+                scale(s, t, h, inner(s, t, h))
+            if h == 0:
+                for t in range(TILES):
+                    before = keep(blocks[s, t, pl.ds(0, LEN), :], at < tab[s, t])
+                    after = keep(blocks[s, t + 1, pl.ds(0, LEN), :], at >= tab[s, t + 1])
+                    vpair[t] = jnp.concatenate([before, before, after, after], axis=1)
+            for t in range(1, TILES - 1):
+                apply(s, t, h)
+        for h in range(len(halves)):
+            finish(s, h)
         return carry
 
     lax.fori_loop(0, SWEEPS, sweep, 0)
-    stores = pltpu.make_async_copy(x, out, store_sem)
-    stores.start()
-    stores.wait()
 
 
 def tables(offsets, owners):
@@ -239,29 +260,30 @@
     dma = pltpu.SemaphoreType.DMA
     n_ring = nz - 1
     return pl.pallas_call(
-        functools.partial(kernel, nx, nz, nrow),
-        out_shape=jax.ShapeDtypeStruct(slab.shape, F32),
+        functools.partial(kernel, nx, nz, nrow, 384),
+        out_shape=pltpu.VMEM(slab.shape, F32),
         in_specs=[
             pl.BlockSpec(memory_space=pltpu.SMEM),
             pl.BlockSpec(memory_space=pl.ANY),
             pl.BlockSpec(memory_space=pltpu.VMEM),
             pl.BlockSpec(memory_space=pltpu.VMEM),
         ],
-        out_specs=pl.BlockSpec(memory_space=pl.ANY),
+        out_specs=pl.BlockSpec(memory_space=pltpu.VMEM),
         scratch_shapes=[
-            pltpu.VMEM(slab.shape, F32),
             pltpu.VMEM((SWEEPS, BLK, NB), BF16),
             pltpu.VMEM((ncol, BLK // nz, NB), BF16),
             pltpu.VMEM((nx, SLOTS, BLK, NB), BF16),
             pltpu.VMEM((SLOTS, NB, LEN), BF16),
-            pltpu.VMEM((2, NB, cols), F32),
+            pltpu.VMEM((TILES, LEN, 4 * NB), BF16),
+            pltpu.VMEM((SLOTS, 2 * NB, cols), BF16),
             pltpu.VMEM((2, 2, NB, cols), F32),
-            dma, dma, dma((2,)),
+            pltpu.VMEM((2, 2, NB, cols), F32),
+            dma, dma((2,)),
             dma((n_ring,)), dma((n_ring,)),
             dma((4,)), dma((4,)),
             dma((nx - 1,)), dma((nx - 1,)),
             dma((n_ring,)), dma((n_ring,)),
-            dma((2,)), dma((2, 2)),
+            dma((2, 2, 2)), dma((2, 2, 2)),
         ],
         compiler_params=pltpu.CompilerParams(
             collective_id=0, has_side_effects=True, vmem_limit_bytes=56 * 2**20

time: 92.6 us -> 86.9 us (0.938)
  Pallas kernels: 84.2 us -> 80.9 us
  local copies, waits for them, and re-layouts: 4.36 us -> 2 us
    pallas_call x1, Pallas kernels: 84.2 us -> 80.9 us  [on_device(): pl.pallas_call(functools.partial(kernel, nx, nz, nrow, 384), out_shape=pl...]
    unnamed x1, local copies, waits for them, and re-layouts: 4.29 us -> 1.93 us
where the time goes in v2:
time: 86.9 us; the launch traced here: 85.4 us
  Pallas kernels  80.9 us (93%)
  other arithmetic  2.51 us (3%)
  local copies, waits for them, and re-layouts  2 us (2%)
    pallas_call x1, Pallas kernels, on_device(): pl.pallas_call(functools.partial(kernel, nx, nz, nrow, 384), out_shape=pl...  80.9 us
    unnamed x1, local copies, waits for them, and re-layouts  1.93 us

profile of v2, /device:TPU:1, one launch (start us, length us, event | category | flops | bytes accessed | tf_op | source)
XLA Modules:
  0.0 85.4 jit_solution(9265521687504678098)
XLA Ops:
  0.0 0.8 add_select_fusion.1
  0.8 1.0 %fusion = (s32[4,8]{1,0:T(4,128)S(1)}, s32[4,8]{1,0:T(4,128)S(1)}, s32[4,8]{1,0:T(4,128)S(1)}) fusion(s32[4,32]{1,0:T(4,128)S(1)} %get-tuple-element.10, s32[4,32]{1,0:T(4,128)S(1)} %get-tuple-element.8, s32[8]{0:T(128)S(1)} %compare_select_fusion.2, s32[4,32]{1,0:T(4,128)} %param.9), kind=kLoop, calls=%fused_computation.3 | loop fusion | flops 7072 | bytes 1952 | tf_op jit(solution)/shard_map/reduce_sum | solution.py:248
  1.9 0.1 broadcast_in_dim.7
  1.9 0.7 pad_add_fusion.tab
  2.6 80.9 %shard_map.55 = f32[1536,640]{1,0:T(8,128)S(1)} custom-call(s32[4,32]{1,0:T(4,128)} %pad_add_fusion.tab, f32[1536,640]{1,0:T(8,128)} %slab.1, bf16[4,1,256,128]{3,2,1,0:T(8,128)(2,1)} %refl.1, bf16[4,1,128,128]{3,2,1,0:T(8,128)(2,1)} %fact.1), custom_call_target="tpu_custom_call" | custom-call | flops 6000000000 | bytes 9000000 | tf_op jit(solution)/shard_map/pallas_call | solution.py:262
  83.5 1.9 %copy.7 = f32[1536,640]{1,0:T(8,128)} copy(f32[1536,640]{1,0:T(8,128)S(1)} %shard_map.55) | data formatting | bytes 7864320
  (1 shorter events, 0.0 us)

commit v3 on v2

--- a/solution.py
+++ b/solution.py
@@ -14,6 +14,7 @@
 TILES = 6
 ZX = 4
 BLK = LEN + NB
+CUT = 384
 MESH = pl.DeviceIdType.MESH
 F32 = jnp.float32
 BF16 = jnp.bfloat16
@@ -30,7 +31,7 @@
 
 
 def kernel(nx, nz, nrow, cut, tab, slab, refl, fact, x, own, pieces, blocks, vt, vpair, ys, wbuf, wrec,
-           load_sem, a2a_sem, zx_send, zx_recv, xs_send, xs_recv, xz_send, xz_recv, zs_send, zs_recv,
+           load_sem, a2a_sem, zx_send, zx_recv, xs_send, xs_recv, far_send, far_recv, xz_send, xz_recv, zs_send, zs_recv,
            w_send, w_recv):
     ncol = nx * nz
     me = lax.axis_index("col")
@@ -98,68 +99,83 @@
     first = pl.ds(0, ZX)
     second = pl.ds(ZX, SLOTS - ZX)
     n_cw, n_ccw = nz // 2, (nz - 1) // 2
+    reach = [0] + [-1 - k for k in range(n_cw)] + [1 + k for k in range(n_ccw)]
     sent = []
 
-    def zx_step(k, way):
-        part = blocks.at[mx, first, rows_of(mz - way * k), :]
-        i = k if way > 0 else n_cw + k
-        copy = move(part, col_of(mx, mz + way), zx_send.at[i], zx_recv.at[i])
+    def start(part, to, send, recv):
+        copy = move(part, to, send, recv)
         sent.append(copy)
         return copy
 
-    def zs_step(k, way):
-        part = blocks.at[:, second, rows_of(mz - way * k), :]
+    def zx_step(k, way):
         i = k if way > 0 else n_cw + k
-        copy = move(part, col_of(mx, mz + way), zs_send.at[i], zs_recv.at[i])
-        sent.append(copy)
-        return copy
+        return start(blocks.at[mx, first, rows_of(mz - way * k), :], col_of(mx, mz + way), zx_send.at[i], zx_recv.at[i])
+
+    def zs_step(k, way, c):
+        i = k if way > 0 else n_cw + k
+        part = blocks.at[c, second, rows_of(mz - way * k), :]
+        return start(part, col_of(mx, mz + way), zs_send.at[i, c], zs_recv.at[i, c])
+
+    near = [[None] * nz, [None] * nz]
+
+    def near_step(i):
+        part = blocks.at[mx, first, rows_of(mz + reach[i]), :]
+        for side, way in ((0, 1), (1, -1)):
+            near[side][i] = start(part, col_of(mx + way, mz), xs_send.at[side, i], xs_recv.at[side, i])
+
+    order = [0] + [i for k in range(n_cw) for i in ((1 + k, 1 + n_cw + k) if k < n_ccw else (1 + k,))]
+    far = []
+
+    def far_step(j):
+        for side, way in ((0, 1), (1, -1)):
+            i = order[2 * j + side]
+            near[side][i].wait_recv()
+            near[side][i] = None
+            part = blocks.at[(mx - way + nx) % nx, first, rows_of(mz + reach[i]), :]
+            far.append(start(part, col_of(mx + way, mz), far_send.at[2 * j + side], far_recv.at[2 * j + side]))
 
     mine = blocks.at[mx, second, my_rows, :]
-    xz = [move(mine, col_of(mx + k, mz), xz_send.at[k - 1], xz_recv.at[k - 1]) for k in range(1, nx)]
-    sent.extend(xz)
+    xz = [start(mine, col_of(mx + k, mz), xz_send.at[k - 1], xz_recv.at[k - 1]) for k in range(1, nx)]
     cw = zx_step(0, 1)
     ccw = zx_step(0, -1) if n_ccw else None
+    near_step(0)
     for copy in xz:
         copy.wait_recv()
-    zcw = zs_step(0, 1)
-    zccw = zs_step(0, -1) if n_ccw else None
+    zcw, zccw = [None] * nx, [None] * nx
+    for c in range(nx):
+        zcw[c] = zs_step(0, 1, c)
+        if n_ccw:
+            zccw[c] = zs_step(0, -1, c)
     for k in range(n_cw):
         cw.wait_recv()
         if k + 1 < n_cw:
             cw = zx_step(k + 1, 1)
+        near_step(1 + k)
         if k < n_ccw:
             ccw.wait_recv()
             if k + 1 < n_ccw:
                 ccw = zx_step(k + 1, -1)
-    xs = [
-        move(blocks.at[mx, first], col_of(mx + way, mz), xs_send.at[i], xs_recv.at[i])
-        for i, way in enumerate((1, -1))
-    ]
-    sent.extend(xs)
-    half = ZX // 2
-    far = []
-    for k in range(n_cw):
-        zcw.wait_recv()
-        if k + 1 < n_cw:
-            zcw = zs_step(k + 1, 1)
-        if k < n_ccw:
-            zccw.wait_recv()
-            if k + 1 < n_ccw:
-                zccw = zs_step(k + 1, -1)
-        if k == n_cw // 2:
-            for i, way in enumerate((1, -1)):
-                xs[i].wait_recv()
-                part = blocks.at[(mx - way + nx) % nx, pl.ds(i * half, half)]
-                far.append(move(part, col_of(mx + way, mz), xs_send.at[2 + i], xs_recv.at[2 + i]))
-    sent.extend(far)
-    for copy in far:
-        copy.wait_recv()
+            near_step(1 + n_cw + k)
+        if k > 0:
+            far_step(k - 1)
+        for c in range(nx):
+            zcw[c].wait_recv()
+            if k + 1 < n_cw:
+                zcw[c] = zs_step(k + 1, 1, c)
+            if k < n_ccw:
+                zccw[c].wait_recv()
+                if k + 1 < n_ccw:
+                    zccw[c] = zs_step(k + 1, -1, c)
+    far_step(n_cw - 1)
+    for copy in near[0] + near[1] + far:
+        if copy is not None:
+            copy.wait_recv()
     for copy in sent:
         copy.wait_send()
     loads.wait()
 
     at = lax.broadcasted_iota(jnp.int32, (LEN, 1), 0)
-    halves = [(0, cut), (cut, cols - cut)] if cut < cols else [(0, cols)]
+    halves = [(at0, min(cut, cols - at0)) for at0 in range(0, cols, cut)]
 
     def keep(value, mask):
         return jnp.where(mask, value.astype(F32), 0.0).astype(BF16)
@@ -176,16 +192,16 @@
         else:
             z = jnp.where(at >= d, tile(t - 1, h), tile(t, h))
         high, low = split(z)
-        return dot(vt[t], high) + dot(vt[t], low)
+        return dot(vt[s % 2, t], high) + dot(vt[s % 2, t], low)
 
     def scale(s, t, h, w):
         f = blocks[s, t, pl.ds(LEN, NB), :]
         y = dot(jnp.concatenate([f, f], axis=1), jnp.concatenate(split(w), axis=0))
-        ys[t, :, pl.ds(*halves[h])] = jnp.concatenate(split(y), axis=0)
+        ys[s % 2, t, :, pl.ds(*halves[h])] = jnp.concatenate(split(y), axis=0)
 
     def apply(s, t, h):
         here = pl.ds(t * LEN, LEN), pl.ds(*halves[h])
-        delta = dot(vpair[t], ys[pl.ds(t, 2), :, pl.ds(*halves[h])].reshape(4 * NB, halves[h][1]))
+        delta = dot(vpair[s % 2, t], ys[s % 2, pl.ds(t, 2), :, pl.ds(*halves[h])].reshape(4 * NB, halves[h][1]))
         x[here] = x[here] - delta
 
     def exchange(s, h):
@@ -214,25 +230,36 @@
         apply(s, 0, h)
         apply(s, TILES - 1, h)
 
+    def begin(s):
+        for t in range(SLOTS):
+            vt[s % 2, t] = blocks[s, t, pl.ds(0, LEN), :].T
+        for t in range(TILES):
+            before = keep(blocks[s, t, pl.ds(0, LEN), :], at < tab[s, t])
+            after = keep(blocks[s, t + 1, pl.ds(0, LEN), :], at >= tab[s, t + 1])
+            vpair[s % 2, t] = jnp.concatenate([before, before, after, after], axis=1)
+
+    def interior(s, h):
+        for t in range(1, SLOTS - 1):
+            scale(s, t, h, inner(s, t, h))
+        for t in range(1, TILES - 1):
+            apply(s, t, h)
+
+    begin(0)
+    for h in range(len(halves)):
+        edges(0, h)
+        interior(0, h)
+
     def sweep(s, carry):
-        for t in range(SLOTS):
-            vt[t] = blocks[s, t, pl.ds(0, LEN), :].T
+        begin(s)
         for h in range(len(halves)):
+            finish(s - 1, h)
             edges(s, h)
-            for t in range(1, SLOTS - 1):
-                scale(s, t, h, inner(s, t, h))
-            if h == 0:
-                for t in range(TILES):
-                    before = keep(blocks[s, t, pl.ds(0, LEN), :], at < tab[s, t])
-                    after = keep(blocks[s, t + 1, pl.ds(0, LEN), :], at >= tab[s, t + 1])
-                    vpair[t] = jnp.concatenate([before, before, after, after], axis=1)
-            for t in range(1, TILES - 1):
-                apply(s, t, h)
-        for h in range(len(halves)):
-            finish(s, h)
+            interior(s, h)
         return carry
 
-    lax.fori_loop(0, SWEEPS, sweep, 0)
+    lax.fori_loop(1, SWEEPS, sweep, 0)
+    for h in range(len(halves)):
+        finish(SWEEPS - 1, h)
 
 
 def tables(offsets, owners):
@@ -259,8 +286,9 @@
     ncol = nx * nz
     dma = pltpu.SemaphoreType.DMA
     n_ring = nz - 1
+    n_group = -(-cols // CUT)
     return pl.pallas_call(
-        functools.partial(kernel, nx, nz, nrow, 384),
+        functools.partial(kernel, nx, nz, nrow, CUT),
         out_shape=pltpu.VMEM(slab.shape, F32),
         in_specs=[
             pl.BlockSpec(memory_space=pltpu.SMEM),
@@ -273,17 +301,18 @@
             pltpu.VMEM((SWEEPS, BLK, NB), BF16),
             pltpu.VMEM((ncol, BLK // nz, NB), BF16),
             pltpu.VMEM((nx, SLOTS, BLK, NB), BF16),
-            pltpu.VMEM((SLOTS, NB, LEN), BF16),
-            pltpu.VMEM((TILES, LEN, 4 * NB), BF16),
-            pltpu.VMEM((SLOTS, 2 * NB, cols), BF16),
+            pltpu.VMEM((2, SLOTS, NB, LEN), BF16),
+            pltpu.VMEM((2, TILES, LEN, 4 * NB), BF16),
+            pltpu.VMEM((2, SLOTS, 2 * NB, cols), BF16),
             pltpu.VMEM((2, 2, NB, cols), F32),
             pltpu.VMEM((2, 2, NB, cols), F32),
             dma, dma((2,)),
             dma((n_ring,)), dma((n_ring,)),
-            dma((4,)), dma((4,)),
+            dma((2, nz)), dma((2, nz)),
+            dma((nz,)), dma((nz,)),
             dma((nx - 1,)), dma((nx - 1,)),
-            dma((n_ring,)), dma((n_ring,)),
-            dma((2, 2, 2)), dma((2, 2, 2)),
+            dma((n_ring, nx)), dma((n_ring, nx)),
+            dma((2, 2, n_group)), dma((2, 2, n_group)),
         ],
         compiler_params=pltpu.CompilerParams(
             collective_id=0, has_side_effects=True, vmem_limit_bytes=56 * 2**20

time: 86.9 us -> 79.8 us (0.918); the launches traced: 85.4 us -> 79.7 us
  Pallas kernels: 80.9 us -> 75.2 us
    pallas_call x1, Pallas kernels: 80.9 us -> 75.2 us  [on_device(): pl.pallas_call(functools.partial(kernel, nx, nz, nrow, CUT), out_shape=pl...]
where the time goes in v3:
time: 79.8 us; the launch traced here: 79.7 us
  Pallas kernels  75.2 us (94%)
  other arithmetic  2.51 us (3%)
  local copies, waits for them, and re-layouts  2 us (3%)
    pallas_call x1, Pallas kernels, on_device(): pl.pallas_call(functools.partial(kernel, nx, nz, nrow, CUT), out_shape=pl...  75.2 us
    unnamed x1, local copies, waits for them, and re-layouts  1.93 us

profile of v3, /device:TPU:1, one launch (start us, length us, event | category | flops | bytes accessed | tf_op | source)
XLA Modules:
  0.0 79.7 jit_solution(14594535932370574667)
XLA Ops:
  0.0 0.8 %add_select_fusion.1 = (s32[4,32]{1,0:T(4,128)S(1)}, s32[4]{0:T(128)S(1)}, s32[4,32]{1,0:T(4,128)S(1)}) fusion(s32[4,32]{1,0:T(4,128)} %param.8, s32[4,32]{1,0:T(4,128)} %param.9, s32[]{:T(128)S(6)} %axis_index.25), kind=kLoop, calls=%fused_computation.7 | loop fusion | flops 2812 | bytes 2068 | tf_op jit(solution)/shard_map/jit(floor_divide)/jit(_where)/select_n | solution.py:267
  0.8 1.0 %fusion = (s32[4,8]{1,0:T(4,128)S(1)}, s32[4,8]{1,0:T(4,128)S(1)}, s32[4,8]{1,0:T(4,128)S(1)}) fusion(s32[4,32]{1,0:T(4,128)S(1)} %get-tuple-element.10, s32[4,32]{1,0:T(4,128)S(1)} %get-tuple-element.8, s32[8]{0:T(128)S(1)} %compare_select_fusion.2, s32[4,32]{1,0:T(4,128)} %param.9), kind=kLoop, calls=%fused_computation.3 | loop fusion | flops 7072 | bytes 1952 | tf_op jit(solution)/shard_map/reduce_sum | solution.py:275
  1.9 0.1 broadcast_in_dim.7
  1.9 0.7 pad_add_fusion.tab
  2.6 75.2 %shard_map.55 = f32[1536,640]{1,0:T(8,128)S(1)} custom-call(s32[4,32]{1,0:T(4,128)} %pad_add_fusion.tab, f32[1536,640]{1,0:T(8,128)} %slab.1, bf16[4,1,256,128]{3,2,1,0:T(8,128)(2,1)} %refl.1, bf16[4,1,128,128]{3,2,1,0:T(8,128)(2,1)} %fact.1), custom_call_target="tpu_custom_call" | custom-call | flops 6000000000 | bytes 9000000 | tf_op jit(solution)/shard_map/pallas_call | solution.py:290
  77.8 1.9 %copy.7 = f32[1536,640]{1,0:T(8,128)} copy(f32[1536,640]{1,0:T(8,128)S(1)} %shard_map.55) | data formatting | bytes 7864320
  (1 shorter events, 0.0 us)

commit v4 on v3

--- a/solution.py
+++ b/solution.py
@@ -14,7 +14,7 @@
 TILES = 6
 ZX = 4
 BLK = LEN + NB
-CUT = 384
+CUT = 256
 MESH = pl.DeviceIdType.MESH
 F32 = jnp.float32
 BF16 = jnp.bfloat16
@@ -30,8 +30,8 @@
     return jnp.dot(left, right, preferred_element_type=F32)
 
 
-def kernel(nx, nz, nrow, cut, tab, slab, refl, fact, x, own, pieces, blocks, vt, vpair, ys, wbuf, wrec,
-           load_sem, a2a_sem, zx_send, zx_recv, xs_send, xs_recv, far_send, far_recv, xz_send, xz_recv, zs_send, zs_recv,
+def kernel(nx, nz, nrow, cut, offsets, owners, slab, refl, fact, x, tab, own, pieces, other, blocks, vt, vpair, ys, wbuf, wrec,
+           load_sem, a2a_sem, pair_sem, zx_send, zx_recv, xs_send, xs_recv, far_send, far_recv, xz_send, xz_recv, zs_send, zs_recv,
            w_send, w_recv):
     ncol = nx * nz
     me = lax.axis_index("col")
@@ -56,33 +56,80 @@
     ri = lax.broadcasted_iota(jnp.int32, (LEN, LEN), 0)
     ci = lax.broadcasted_iota(jnp.int32, (LEN, LEN), 1)
     for s in range(SWEEPS):
-        place = (((ri - tab[s, 24]) & (LEN - 1)) == ci).astype(BF16)
+        held = jnp.sum(jnp.where(owners[pl.ds(s, 1), :] == me, offsets[pl.ds(s, 1), :] & (LEN - 1), 0))
+        place = (((ri - held) & (LEN - 1)) == ci).astype(BF16)
         own[s, pl.ds(0, LEN), :] = dot(place, refl[s, 0]).astype(BF16)
         own[s, pl.ds(LEN, NB), :] = fact[s, 0]
 
+    def slot_of(s, t, of_row, value):
+        begins_here = offsets[pl.ds(s, 1), :] // LEN == of_row * TILES + (t - 1)
+        return jnp.sum(jnp.where(begins_here, value(pl.ds(s, 1)), 0))
+
+    def within(s):
+        return offsets[s, :] & (LEN - 1)
+
+    def holder(s):
+        return owners[s, :] + ncol
+
+    for s in range(SWEEPS):
+        for t in range(SLOTS):
+            tab[s, t] = slot_of(s, t, row, within)
+    core = row % 2
+    sibling = row + 1 - 2 * core
+    wanted = [[slot_of(mx, t, of_row, holder) for t in range(SLOTS)] for of_row in (row, sibling)]
+
     pl.semaphore_wait(barrier, ncol + 1)
+    sender = mz % 2 == core
 
     def send_piece(k, carry):
         to = (me + k) % ncol
         pltpu.make_async_remote_copy(
             src_ref=own.at[to // nz, pl.ds(pl.multiple_of((to % nz) * piece, 16), piece), :],
-            dst_ref=pieces.at[me],
-            send_sem=a2a_sem.at[0],
+            dst_ref=pieces.at[me // 2],
+            send_sem=a2a_sem.at[2 * (k // pieces.shape[0])],
             recv_sem=a2a_sem.at[1],
             device_id={"col": to},
             device_id_type=MESH,
         ).start()
         return carry
 
-    lax.fori_loop(1, ncol, send_piece, 0)
     my_rows = pl.ds(pl.multiple_of(mz * piece, 16), piece)
-    pieces[me] = own[mx, my_rows, :]
-    everything = pieces.at[pl.ds(0, ncol - 1)]
-    pltpu.make_async_copy(everything, everything, a2a_sem.at[1]).wait()
+    n_sent = pieces.shape[0]
+
+    def await_pieces(count, sem):
+        some = pieces.at[pl.ds(0, count)]
+        pltpu.make_async_copy(some, some, sem).wait()
+
+    @pl.when(sender)
+    def _():
+        lax.fori_loop(1, ncol, send_piece, 0)
+        pieces[me // 2] = own[mx, my_rows, :]
+        await_pieces(n_sent - 1, a2a_sem.at[1])
+
+    @pl.when(jnp.logical_not(sender))
+    def _():
+        await_pieces(n_sent, a2a_sem.at[1])
+
+    def found(at_holder):
+        here = jnp.logical_and(at_holder >= ncol, at_holder % 2 == core)
+        return pieces[(at_holder % ncol) // 2].astype(F32) * here.astype(F32)
+
     for t in range(SLOTS):
-        found = pieces[tab[mx, 8 + t]].astype(F32) * tab[mx, 16 + t].astype(F32)
-        blocks[mx, t, my_rows, :] = found.astype(BF16)
-    pltpu.make_async_copy(everything, everything, a2a_sem.at[0]).wait()
+        other[0, t] = found(wanted[1][t]).astype(BF16)
+    handed = pltpu.make_async_remote_copy(
+        src_ref=other.at[0], dst_ref=other.at[1], send_sem=pair_sem.at[0], recv_sem=pair_sem.at[1],
+        device_id={"row": sibling}, device_id_type=MESH)
+    handed.start()
+    mine_found = [found(wanted[0][t]) for t in range(SLOTS)]
+    handed.wait_recv()
+    for t in range(SLOTS):
+        blocks[mx, t, my_rows, :] = (mine_found[t] + other[1, t].astype(F32)).astype(BF16)
+    handed.wait_send()
+
+    @pl.when(sender)
+    def _():
+        await_pieces(n_sent - 1, a2a_sem.at[0])
+        await_pieces(n_sent, a2a_sem.at[2])
 
     def col_of(cx, cz):
         return ((cx + nx) % nx) * nz + (cz + nz) % nz
@@ -191,13 +238,15 @@
             z = jnp.where(at >= d, tile(TILES - 1, h), 0.0)
         else:
             z = jnp.where(at >= d, tile(t - 1, h), tile(t, h))
-        high, low = split(z)
-        return dot(vt[s % 2, t], high) + dot(vt[s % 2, t], low)
-
-    def scale(s, t, h, w):
-        f = blocks[s, t, pl.ds(LEN, NB), :]
-        y = dot(jnp.concatenate([f, f], axis=1), jnp.concatenate(split(w), axis=0))
-        ys[s % 2, t, :, pl.ds(*halves[h])] = jnp.concatenate(split(y), axis=0)
+        return dot(vt[s % 2, t], jnp.concatenate(split(z), axis=0))
+
+    def scale(s, slots, h, sums):
+        y = []
+        for t, w in zip(slots, sums):
+            f = blocks[s, t, pl.ds(LEN, NB), :]
+            y.append(dot(jnp.concatenate([f, f], axis=1), jnp.concatenate(split(w), axis=0)))
+        for t, value in zip(slots, y):
+            ys[s % 2, t, :, pl.ds(*halves[h])] = jnp.concatenate(split(value), axis=0)
 
     def apply(s, t, h):
         here = pl.ds(t * LEN, LEN), pl.ds(*halves[h])
@@ -216,8 +265,9 @@
         ]
 
     def edges(s, h):
-        wbuf[s % 2, 0, :, pl.ds(*halves[h])] = inner(s, 0, h)
-        wbuf[s % 2, 1, :, pl.ds(*halves[h])] = inner(s, SLOTS - 1, h)
+        first_sum, last_sum = inner(s, 0, h), inner(s, SLOTS - 1, h)
+        wbuf[s % 2, 0, :, pl.ds(*halves[h])] = first_sum
+        wbuf[s % 2, 1, :, pl.ds(*halves[h])] = last_sum
         for copy in exchange(s, h):
             copy.start()
 
@@ -225,22 +275,21 @@
         for copy in exchange(s, h):
             copy.wait()
         part = pl.ds(*halves[h])
-        for side, t in ((0, 0), (1, SLOTS - 1)):
-            scale(s, t, h, wbuf[s % 2, side, :, part] + wrec[s % 2, side, :, part])
+        scale(s, (0, SLOTS - 1), h, [wbuf[s % 2, side, :, part] + wrec[s % 2, side, :, part] for side in (0, 1)])
         apply(s, 0, h)
         apply(s, TILES - 1, h)
 
     def begin(s):
         for t in range(SLOTS):
-            vt[s % 2, t] = blocks[s, t, pl.ds(0, LEN), :].T
+            turned = blocks[s, t, pl.ds(0, LEN), :].T
+            vt[s % 2, t] = jnp.concatenate([turned, turned], axis=1)
         for t in range(TILES):
             before = keep(blocks[s, t, pl.ds(0, LEN), :], at < tab[s, t])
             after = keep(blocks[s, t + 1, pl.ds(0, LEN), :], at >= tab[s, t + 1])
             vpair[s % 2, t] = jnp.concatenate([before, before, after, after], axis=1)
 
     def interior(s, h):
-        for t in range(1, SLOTS - 1):
-            scale(s, t, h, inner(s, t, h))
+        scale(s, range(1, SLOTS - 1), h, [inner(s, t, h) for t in range(1, SLOTS - 1)])
         for t in range(1, TILES - 1):
             apply(s, t, h)
 
@@ -260,25 +309,6 @@
     lax.fori_loop(1, SWEEPS, sweep, 0)
     for h in range(len(halves)):
         finish(SWEEPS - 1, h)
-
-
-def tables(offsets, owners):
-    row, col = lax.axis_index("row"), lax.axis_index("col")
-    begin_tile = offsets // LEN
-    within = offsets % LEN
-    slot = jnp.arange(8, dtype=jnp.int32) + (row * TILES - 1)
-    slot = jnp.where(jnp.arange(8) < SLOTS, slot, -2)
-    match = (begin_tile[:, None, :] == slot[None, :, None]).astype(jnp.int32)
-    own = jnp.sum((owners == col) * within, axis=1, keepdims=True)
-    return jnp.concatenate(
-        [
-            jnp.sum(match * within[:, None, :], axis=2),
-            jnp.sum(match * owners[:, None, :], axis=2),
-            jnp.sum(match, axis=2),
-            jnp.broadcast_to(own, (SWEEPS, 8)),
-        ],
-        axis=1,
-    ).astype(jnp.int32)
 
 
 def on_device(nx, nz, nrow, slab, reflectors, factors, offsets, owners):
@@ -291,22 +321,25 @@
         functools.partial(kernel, nx, nz, nrow, CUT),
         out_shape=pltpu.VMEM(slab.shape, F32),
         in_specs=[
-            pl.BlockSpec(memory_space=pltpu.SMEM),
+            pl.BlockSpec(memory_space=pltpu.VMEM),
+            pl.BlockSpec(memory_space=pltpu.VMEM),
             pl.BlockSpec(memory_space=pl.ANY),
             pl.BlockSpec(memory_space=pltpu.VMEM),
             pl.BlockSpec(memory_space=pltpu.VMEM),
         ],
         out_specs=pl.BlockSpec(memory_space=pltpu.VMEM),
         scratch_shapes=[
+            pltpu.SMEM((SWEEPS, 8), jnp.int32),
             pltpu.VMEM((SWEEPS, BLK, NB), BF16),
-            pltpu.VMEM((ncol, BLK // nz, NB), BF16),
+            pltpu.VMEM((ncol // 2, BLK // nz, NB), BF16),
+            pltpu.VMEM((2, SLOTS, BLK // nz, NB), BF16),
             pltpu.VMEM((nx, SLOTS, BLK, NB), BF16),
-            pltpu.VMEM((2, SLOTS, NB, LEN), BF16),
+            pltpu.VMEM((2, SLOTS, NB, 2 * LEN), BF16),
             pltpu.VMEM((2, TILES, LEN, 4 * NB), BF16),
             pltpu.VMEM((2, SLOTS, 2 * NB, cols), BF16),
             pltpu.VMEM((2, 2, NB, cols), F32),
             pltpu.VMEM((2, 2, NB, cols), F32),
-            dma, dma((2,)),
+            dma, dma((3,)), dma((2,)),
             dma((n_ring,)), dma((n_ring,)),
             dma((2, nz)), dma((2, nz)),
             dma((nz,)), dma((nz,)),
@@ -318,7 +351,7 @@
             collective_id=0, has_side_effects=True, vmem_limit_bytes=56 * 2**20
         ),
         cost_estimate=pl.CostEstimate(flops=6_000_000_000, bytes_accessed=9_000_000, transcendentals=0),
-    )(tables(offsets, owners), slab, reflectors, factors)
+    )(offsets, owners, slab, reflectors, factors)
 
 
 def solution(mesh):

time: 79.8 us -> 73.7 us (0.924)
  Pallas kernels: 75.2 us -> 71.6 us
  other arithmetic: 2.51 us -> 0 us
    pallas_call x1, Pallas kernels: 75.2 us -> 71.6 us  [on_device(): pl.pallas_call(functools.partial(kernel, nx, nz, nrow, CUT), out_shape=pl...]
    reduce_sum x1 -> x0, other arithmetic: 1.03 us -> none  [tables(): jnp.sum(match * within[:, None, :], axis=2)]
    select_n x2 -> x0, other arithmetic: 0.82 us -> none  [the longest x1 0.82 us: tables(): begin_tile = offsets // LEN]
where the time goes in v4:
time: 73.7 us; the launch traced here: 73.6 us
  Pallas kernels  71.6 us (97%)
  local copies, waits for them, and re-layouts  1.93 us (3%)
    pallas_call x1, Pallas kernels, on_device(): pl.pallas_call(functools.partial(kernel, nx, nz, nrow, CUT), out_shape=pl...  71.6 us
    unnamed x1, local copies, waits for them, and re-layouts  1.93 us

profile of v4, /device:TPU:1, one launch (start us, length us, event | category | flops | bytes accessed | tf_op | source)
XLA Modules:
  0.0 73.6 jit_solution(6140203946710288748)
XLA Ops:
  0.0 71.6 %shard_map.55 = f32[1536,640]{1,0:T(8,128)S(1)} custom-call(s32[4,32]{1,0:T(4,128)} %offsets.1, s32[4,32]{1,0:T(4,128)} %owners.1, f32[1536,640]{1,0:T(8,128)} %slab.1, bf16[4,1,256,128]{3,2,1,0:T(8,128)(2,1)} %refl.1, bf16[4,1,128,128]{3,2,1,0:T(8,128)(2,1)} %fact.1), custom_call_target="tpu_custom_call" | custom-call | flops 6000000000 | bytes 9000000 | tf_op jit(solution)/shard_map/pallas_call | solution.py:320
  71.6 1.9 %copy.7 = f32[1536,640]{1,0:T(8,128)} copy(f32[1536,640]{1,0:T(8,128)S(1)} %shard_map.55) | data formatting | bytes 7864320

commit v5 on v4

--- a/solution.py
+++ b/solution.py
@@ -12,7 +12,7 @@
 NB = 128
 SLOTS = 7
 TILES = 6
-ZX = 4
+ZX = 5
 BLK = LEN + NB
 CUT = 256
 MESH = pl.DeviceIdType.MESH
@@ -217,8 +217,6 @@
     for copy in near[0] + near[1] + far:
         if copy is not None:
             copy.wait_recv()
-    for copy in sent:
-        copy.wait_send()
     loads.wait()
 
     at = lax.broadcasted_iota(jnp.int32, (LEN, 1), 0)
@@ -309,6 +307,8 @@
     lax.fori_loop(1, SWEEPS, sweep, 0)
     for h in range(len(halves)):
         finish(SWEEPS - 1, h)
+    for copy in sent:
+        copy.wait_send()
 
 
 def on_device(nx, nz, nrow, slab, reflectors, factors, offsets, owners):

time: 73.7 us -> 71.6 us (0.972)
  Pallas kernels: 71.6 us -> 69.5 us
    pallas_call x1, Pallas kernels: 71.6 us -> 69.5 us  [on_device(): pl.pallas_call(functools.partial(kernel, nx, nz, nrow, CUT), out_shape=pl...]
where the time goes in v5:
time: 71.6 us; the launch traced here: 71.5 us
  Pallas kernels  69.5 us (97%)
  local copies, waits for them, and re-layouts  1.93 us (3%)
    pallas_call x1, Pallas kernels, on_device(): pl.pallas_call(functools.partial(kernel, nx, nz, nrow, CUT), out_shape=pl...  69.5 us
    unnamed x1, local copies, waits for them, and re-layouts  1.93 us

profile of v5, /device:TPU:1, one launch (start us, length us, event | category | flops | bytes accessed | tf_op | source)
XLA Modules:
  0.0 71.5 jit_solution(4237253296739409399)
XLA Ops:
  0.0 69.5 %shard_map.55 = f32[1536,640]{1,0:T(8,128)S(1)} custom-call(s32[4,32]{1,0:T(4,128)} %offsets.1, s32[4,32]{1,0:T(4,128)} %owners.1, f32[1536,640]{1,0:T(8,128)} %slab.1, bf16[4,1,256,128]{3,2,1,0:T(8,128)(2,1)} %refl.1, bf16[4,1,128,128]{3,2,1,0:T(8,128)(2,1)} %fact.1), custom_call_target="tpu_custom_call" | custom-call | flops 6000000000 | bytes 9000000 | tf_op jit(solution)/shard_map/pallas_call | solution.py:320
  69.5 1.9 %copy.7 = f32[1536,640]{1,0:T(8,128)} copy(f32[1536,640]{1,0:T(8,128)S(1)} %shard_map.55) | data formatting | bytes 7864320
